TPU v7x, 32 devices: a whole 2x2x4 slice. The times are simulated.
32 devices in a mesh: dp: 8 (over z, y), tensor: 4 (over x, core).
Axes of the slice: x: 2, y: 2, z: 4, core: 2. Of those that a mesh axis runs over, the one named last changes fastest.
Arguments:
- block_input: bfloat16 [8, 4096, 768], P('dp', 'tensor'), may hold values from -8 to 8
- output_grad: bfloat16 [8, 4096, 768], P('dp', 'tensor'), may hold values from -6 to 6
- segments: int32 [8, 4096], P('dp', 'tensor'), may hold values from 0 to 3, never falling along the last dimension, each value on 1 to 2000 neighbouring positions
- inner_proj: float32 [768, 2, 1536], P('dp', None, 'tensor'), may hold values from -0.21875 to 0.21875
- inner_first: float32 [768, 2, 1536], P('dp', None, 'tensor'), may hold values from -64 to 64
- inner_second: float32 [768, 2, 1536], P('dp', None, 'tensor'), may hold values from 8.192 to 32.768
- step_proj: float32 [768, 24], P('dp', 'tensor'), may hold values from -0.21875 to 0.21875
- step_first: float32 [768, 24], P('dp', 'tensor'), may hold values from -6 to 6
- step_second: float32 [768, 24], P('dp', 'tensor'), may hold values from 0.08192 to 0.32768
- state_proj: float32 [768, 256], P('dp'), may hold values from -0.21875 to 0.21875
- state_first: float32 [768, 256], P('dp'), may hold values from -32 to 32
- state_second: float32 [768, 256], P('dp'), may hold values from 2.94912 to 11.79648
- outer_proj: float32 [768, 1536], P('dp', 'tensor'), may hold values from -0.15625 to 0.15625
- outer_first: float32 [768, 1536], P('dp', 'tensor'), may hold values from -128 to 128
- outer_second: float32 [768, 1536], P('dp', 'tensor'), may hold values from 32.768 to 131.072
- channel_params: float32 [6, 1536], P(None, 'tensor'), may hold values from -0.75 to 2.5
- channel_first: float32 [6, 1536], P(None, 'tensor'), may hold values from -64 to 64
- channel_second: float32 [6, 1536], P(None, 'tensor'), may hold values from 8.192 to 32.768
- head_params: float32 [3, 24], P(None, 'tensor'), may hold values from -6.5 to 2.7
- head_first: float32 [3, 24], P(None, 'tensor'), may hold values from -64 to 64
- head_second: float32 [3, 24], P(None, 'tensor'), may hold values from 8.192 to 32.768
- state_filter: float32 [5, 256], replicated, may hold values from -0.5 to 0.5
- filter_first: float32 [5, 256], replicated, may hold values from -128 to 128
- filter_second: float32 [5, 256], replicated, may hold values from 32.768 to 131.072
- input_gain: float32 [768], replicated, may hold values from 0.5 to 1.5
- gain_first: float32 [768], replicated, may hold values from -80 to 80
- gain_second: float32 [768], replicated, may hold values from 16.384 to 65.536
Outputs:
- block_output: float32 [8, 4096, 768], P('dp', 'tensor')
- input_grad: float32 [8, 4096, 768], P('dp', 'tensor')
- inner_moment: float32 [768, 2, 1536], P('dp', None, 'tensor')
- inner_square: float32 [768, 2, 1536], P('dp', None, 'tensor')
- inner_master: float32 [768, 2, 1536], P('dp', None, 'tensor')
- step_moment: float32 [768, 24], P('dp', 'tensor')
- step_square: float32 [768, 24], P('dp', 'tensor')
- step_master: float32 [768, 24], P('dp', 'tensor')
- state_moment: float32 [768, 256], P('dp')
- state_square: float32 [768, 256], P('dp')
- state_master: float32 [768, 256], P('dp')
- outer_moment: float32 [768, 1536], P('dp', 'tensor')
- outer_square: float32 [768, 1536], P('dp', 'tensor')
- outer_master: float32 [768, 1536], P('dp', 'tensor')
- channel_moment: float32 [6, 1536], P(None, 'tensor')
- channel_square: float32 [6, 1536], P(None, 'tensor')
- channel_master: float32 [6, 1536], P(None, 'tensor')
- head_moment: float32 [3, 24], P(None, 'tensor')
- head_square: float32 [3, 24], P(None, 'tensor')
- head_master: float32 [3, 24], P(None, 'tensor')
- filter_moment: float32 [5, 256], replicated
- filter_square: float32 [5, 256], replicated
- filter_master: float32 [5, 256], replicated
- gain_moment: float32 [768], replicated
- gain_square: float32 [768], replicated
- gain_master: float32 [768], replicated
Inputs may be any that keep to these rules, and one draw needn't show every extreme that they name: `segments`: segment numbers never fall along a sequence; each sequence holds 4 documents, each of 1 to 2000 tokens, one of exactly 2000.
All inputs are finite; a program needn't handle non-finite values.
Results may differ from a plain program's by a relative error of at most 0.006.
The roundings to bfloat16 on the way count: a program that leaves them out, or rounds other values in their place, can miss the bound.
Values may be sent and summed in bfloat16 or wider, within the bound.
A program may use at most 192 MiB of HBM per device.

v0:
```python
from functools import partial

import jax
import jax.numpy as jnp
from jax import lax
from jax.sharding import PartitionSpec as P

SPAN = 256
STEP = 10


NORM_EPS = 1e-05
BETA_ONE = 0.9
BETA_TWO = 0.999
ADAM_EPS = 1e-08
MATRIX_RATE = 0.1
VECTOR_RATE = 0.3
MATRIX_DECAY = 0.1
HIGHEST = lax.Precision.HIGHEST


def matmul(left, right):
    return jnp.dot(left, right, preferred_element_type=jnp.float32)


def contract_rows(left, right):
    return lax.dot_general(
        left, right, (((0,), (0,)), ((), ())), preferred_element_type=jnp.float32
    )


def contract_last(left, right):
    return lax.dot_general(
        left, right, (((left.ndim - 1,), (1,)), ((), ())), preferred_element_type=jnp.float32
    )


def causal_filter(values, filter_taps, filter_bias, segment):
    taps_count = filter_taps.shape[0]
    seq_len = values.shape[-2]
    filtered = filter_bias + filter_taps[taps_count - 1] * values
    for offset in range(1, taps_count):
        leading = [(0, 0)] * (values.ndim - 2)
        shifted = jnp.pad(values, leading + [(offset, 0), (0, 0)])[..., :seq_len, :]
        earlier = jnp.pad(segment, leading + [(offset, 0)], constant_values=-1)[..., :seq_len]
        same_doc = (earlier == segment).astype(values.dtype)
        filtered = filtered + filter_taps[taps_count - 1 - offset] * shifted * same_doc[..., None]
    return filtered


def span_step(rates, skip, carry, pieces):
    carry_state, last_seg = carry
    block_x, block_b, block_c, block_dt, block_seg = pieces
    block_rows = block_seg.shape[0]
    log_decay = jnp.cumsum(block_dt * rates, axis=0)
    positions = jnp.arange(block_rows)
    same_doc = (block_seg[:, None] == block_seg[None, :]) & (
        positions[:, None] >= positions[None, :]
    )
    log_gaps = log_decay.T[:, :, None] - log_decay.T[:, None, :]
    decays = jnp.where(same_doc[None], jnp.exp(jnp.where(same_doc[None], log_gaps, 0.0)), 0.0)
    scores = jnp.dot(block_c, block_b.T, precision=HIGHEST)
    weights = decays * scores[None] * block_dt.T[:, None, :]
    inner_part = jnp.einsum("hts,shp->thp", weights, block_x, precision=HIGHEST)
    carried = jnp.where((block_seg == last_seg)[:, None], jnp.exp(log_decay), 0.0)
    outer_part = (
        jnp.einsum("hpn,tn->thp", carry_state, block_c, precision=HIGHEST) * carried[:, :, None]
    )
    end_seg = block_seg[block_rows - 1]
    tail_weight = (
        jnp.where(
            (block_seg == end_seg)[:, None],
            jnp.exp(log_decay[block_rows - 1][None, :] - log_decay),
            0.0,
        )
        * block_dt
    )
    kept = jnp.where(last_seg == end_seg, jnp.exp(log_decay[block_rows - 1]), 0.0)
    fresh_state = jnp.einsum("th,thp,tn->hpn", tail_weight, block_x, block_b, precision=HIGHEST)
    new_state = carry_state * kept[:, None, None] + fresh_state
    result = inner_part + outer_part + skip[None, :, None] * block_x
    return ((new_state, end_seg), result)


def scan_states(inputs_x, inputs_b, inputs_c, step_sizes, segment, rates, skip):
    seq_len = inputs_x.shape[0]
    blocks = seq_len // SPAN

    def split_blocks(values):
        return values.reshape((blocks, SPAN) + values.shape[1:])

    start = (
        jnp.zeros((inputs_x.shape[1], inputs_x.shape[2], inputs_b.shape[1]), jnp.float32),
        jnp.array(-1, jnp.int32),
    )
    step_fn = jax.checkpoint(partial(span_step, rates, skip))
    final, outputs = lax.scan(
        step_fn,
        start,
        (
            split_blocks(inputs_x),
            split_blocks(inputs_b),
            split_blocks(inputs_c),
            split_blocks(step_sizes),
            split_blocks(segment),
        ),
    )
    return outputs.reshape(inputs_x.shape)


def filter_parts(segment, inner_raw, state_raw, channel_taps, state_taps):
    taps_count = state_taps.shape[0] - 1
    active_inner = jax.nn.silu(
        causal_filter(inner_raw, channel_taps[:taps_count], channel_taps[taps_count], segment)
    )
    active_state = jax.nn.silu(
        causal_filter(state_raw, state_taps[:taps_count], state_taps[taps_count], segment)
    )
    return (active_inner, active_state)


def mixer_part(segment, active_inner, active_state, step_raw, gate_raw, head_vec):
    sequence_count, length, local_inner = active_inner.shape
    heads_here = head_vec.shape[1]
    state_width = active_state.shape[2] // 2
    step_sizes = jax.nn.softplus(step_raw + head_vec[0])
    rates = -jnp.exp(head_vec[1])
    split_inner = active_inner.reshape(
        sequence_count, length, heads_here, local_inner // heads_here
    )

    def one_sequence(pieces):
        return scan_states(
            pieces[0],
            pieces[1][:, :state_width],
            pieces[1][:, state_width:],
            pieces[2],
            pieces[3],
            rates,
            head_vec[2],
        )

    mixed_heads = lax.map(one_sequence, (split_inner, active_state, step_sizes, segment))
    return mixed_heads.reshape(active_inner.shape) * jax.nn.silu(gate_raw)


def adam_update(weight, gradient, moment_one, moment_two, step_rate, decay_rate):
    first_new = BETA_ONE * moment_one + (1.0 - BETA_ONE) * gradient
    second_new = BETA_TWO * moment_two + (1.0 - BETA_TWO) * gradient * gradient
    first_hat = first_new / (1.0 - BETA_ONE**STEP)
    second_hat = second_new / (1.0 - BETA_TWO**STEP)
    weight_new = weight - step_rate * (
        first_hat / (jnp.sqrt(second_hat) + ADAM_EPS) + decay_rate * weight
    )
    return (first_new, second_new, weight_new)


def shards(
    block_input,
    output_grad,
    segments,
    inner_proj,
    inner_first,
    inner_second,
    step_proj,
    step_first,
    step_second,
    state_proj,
    state_first,
    state_second,
    outer_proj,
    outer_first,
    outer_second,
    channel_params,
    channel_first,
    channel_second,
    head_params,
    head_first,
    head_second,
    state_filter,
    filter_first,
    filter_second,
    input_gain,
    gain_first,
    gain_second,
):
    sequence_count, quarter, model_width = block_input.shape
    tensor_size = lax.axis_size("tensor")
    tensor_rank = lax.axis_index("tensor")
    taps_count = state_filter.shape[0] - 1
    inner_weight, step_weight, state_weight, outer_weight = (
        lax.all_gather(inner_proj.astype(jnp.bfloat16), "dp", axis=0, tiled=True),
        lax.all_gather(step_proj.astype(jnp.bfloat16), "dp", axis=0, tiled=True),
        lax.all_gather(state_proj.astype(jnp.bfloat16), "dp", axis=0, tiled=True),
        lax.all_gather(outer_proj.astype(jnp.bfloat16), "dp", axis=0, tiled=True),
    )
    local_inner = inner_weight.shape[2]
    heads_here = step_weight.shape[1]
    state_cols = state_weight.shape[1]
    stream = block_input.astype(jnp.float32)
    row_scale = lax.rsqrt(jnp.mean(stream * stream, -1, keepdims=True) + NORM_EPS)
    unit_rows = stream * row_scale
    normed = (unit_rows * input_gain).astype(jnp.bfloat16)
    seq_rows, segment = (
        lax.all_gather(normed, "tensor", axis=1, tiled=True),
        lax.all_gather(segments, "tensor", axis=1, tiled=True),
    )
    length = seq_rows.shape[1]
    row_count = sequence_count * length
    flat_rows = seq_rows.reshape(row_count, model_width)
    inner_matrix = inner_weight.reshape(model_width, 2 * local_inner)
    mixed_cols = matmul(flat_rows, inner_matrix)
    gate_raw = mixed_cols[:, :local_inner].reshape(sequence_count, length, local_inner)
    inner_raw = mixed_cols[:, local_inner:].reshape(sequence_count, length, local_inner)
    step_raw = matmul(flat_rows, step_weight).reshape(sequence_count, length, heads_here)
    state_raw = matmul(flat_rows, state_weight).reshape(sequence_count, length, state_cols)
    (active_inner, active_state), filter_back = jax.vjp(
        partial(filter_parts, segment),
        inner_raw,
        state_raw,
        channel_params[: taps_count + 1],
        state_filter,
    )
    rounded_inner = lax.optimization_barrier(active_inner.astype(jnp.bfloat16)).astype(jnp.float32)
    rounded_state = lax.optimization_barrier(active_state.astype(jnp.bfloat16)).astype(jnp.float32)
    gated_out, mixer_back = jax.vjp(
        partial(mixer_part, segment), rounded_inner, rounded_state, step_raw, gate_raw, head_params
    )
    squares = lax.psum(jnp.sum(gated_out * gated_out, -1), "tensor")
    inverse = lax.rsqrt(squares / (local_inner * tensor_size) + NORM_EPS)[..., None]
    gate_gain = channel_params[taps_count + 1]
    normed_out = (gated_out * inverse * gate_gain).astype(jnp.bfloat16)
    summed_parts = contract_last(normed_out.reshape(row_count, local_inner), outer_weight).reshape(
        sequence_count, length, model_width
    )
    own_out = lax.psum_scatter(summed_parts, "tensor", scatter_dimension=1, tiled=True)
    block_output = stream + own_out
    back_rows = lax.all_gather(output_grad, "tensor", axis=1, tiled=True).reshape(
        row_count, model_width
    )
    outer_grad = contract_rows(back_rows, normed_out.reshape(row_count, local_inner))
    normed_grad = matmul(back_rows, outer_weight).reshape(sequence_count, length, local_inner)
    scaled_grad = normed_grad * gate_gain
    dot_sums = lax.psum(jnp.sum(scaled_grad * gated_out, -1), "tensor")[..., None]
    gated_grad = inverse * scaled_grad - gated_out * inverse**3 * dot_sums / (
        local_inner * tensor_size
    )
    gain_grad = jnp.sum(normed_grad * gated_out * inverse, axis=(0, 1))
    inner_back, state_back, step_back, gate_back, head_grad = mixer_back(gated_grad)
    state_total = lax.psum(state_back, "tensor")
    inner_pre, state_pre, taps_grad, filter_grad = filter_back((inner_back, state_total))
    both_low = jnp.concatenate([gate_back.astype(jnp.bfloat16), inner_pre.astype(jnp.bfloat16)], -1)
    step_low = step_back.astype(jnp.bfloat16)
    state_low = state_pre.astype(jnp.bfloat16)
    inner_grad = contract_rows(flat_rows, both_low.reshape(row_count, 2 * local_inner)).reshape(
        model_width, 2, local_inner
    )
    step_grad = contract_rows(flat_rows, step_low.reshape(row_count, heads_here))
    state_grad = contract_rows(flat_rows, state_low.reshape(row_count, state_cols))
    summed_grads = contract_last(
        both_low.reshape(row_count, 2 * local_inner), inner_matrix
    ) + contract_last(step_low.reshape(row_count, heads_here), step_weight)
    own_grad = lax.psum_scatter(
        summed_grads.reshape(sequence_count, length, model_width),
        "tensor",
        scatter_dimension=1,
        tiled=True,
    )
    own_state = lax.dynamic_slice_in_dim(state_low, tensor_rank * quarter, quarter, 1)
    own_grad = own_grad + contract_last(own_state, state_weight)
    scaled_in = own_grad * input_gain
    input_grad = output_grad.astype(jnp.float32) + row_scale * (
        scaled_in - unit_rows * jnp.mean(scaled_in * unit_rows, -1, keepdims=True)
    )
    input_gain_grad = jnp.sum(own_grad * unit_rows, axis=(0, 1))
    inner_sum, step_sum, state_sum, outer_sum = (
        lax.psum_scatter(inner_grad, "dp", scatter_dimension=0, tiled=True),
        lax.psum_scatter(step_grad, "dp", scatter_dimension=0, tiled=True),
        lax.psum_scatter(state_grad, "dp", scatter_dimension=0, tiled=True),
        lax.psum_scatter(outer_grad, "dp", scatter_dimension=0, tiled=True),
    )
    channel_grad = jnp.concatenate([taps_grad, gain_grad[None, :]], 0)
    wide_channel = lax.dynamic_update_slice(
        jnp.zeros((channel_grad.shape[0], local_inner * tensor_size), jnp.float32),
        channel_grad,
        (0, tensor_rank * local_inner),
    )
    wide_head = lax.dynamic_update_slice(
        jnp.zeros((head_grad.shape[0], heads_here * tensor_size), jnp.float32),
        head_grad,
        (0, tensor_rank * heads_here),
    )
    leader = (tensor_rank == 0).astype(jnp.float32)
    channel_all, head_all, filter_all, gain_all = lax.psum(
        (wide_channel, wide_head, filter_grad * leader, input_gain_grad), ("dp", "tensor")
    )
    channel_sum = lax.dynamic_slice_in_dim(channel_all, tensor_rank * local_inner, local_inner, 1)
    head_sum = lax.dynamic_slice_in_dim(head_all, tensor_rank * heads_here, heads_here, 1)
    inner_new = adam_update(
        inner_proj, inner_sum, inner_first, inner_second, MATRIX_RATE, MATRIX_DECAY
    )
    step_new = adam_update(step_proj, step_sum, step_first, step_second, MATRIX_RATE, MATRIX_DECAY)
    state_new = adam_update(
        state_proj, state_sum, state_first, state_second, MATRIX_RATE, MATRIX_DECAY
    )
    outer_new = adam_update(
        outer_proj, outer_sum, outer_first, outer_second, MATRIX_RATE, MATRIX_DECAY
    )
    channel_new = adam_update(
        channel_params, channel_sum, channel_first, channel_second, VECTOR_RATE, 0.0
    )
    head_new = adam_update(head_params, head_sum, head_first, head_second, VECTOR_RATE, 0.0)
    filter_new = adam_update(
        state_filter, filter_all, filter_first, filter_second, VECTOR_RATE, 0.0
    )
    gain_new = adam_update(input_gain, gain_all, gain_first, gain_second, VECTOR_RATE, 0.0)
    return (
        block_output,
        input_grad,
        inner_new[0],
        inner_new[1],
        inner_new[2],
        step_new[0],
        step_new[1],
        step_new[2],
        state_new[0],
        state_new[1],
        state_new[2],
        outer_new[0],
        outer_new[1],
        outer_new[2],
        channel_new[0],
        channel_new[1],
        channel_new[2],
        head_new[0],
        head_new[1],
        head_new[2],
        filter_new[0],
        filter_new[1],
        filter_new[2],
        gain_new[0],
        gain_new[1],
        gain_new[2],
    )


def solution(mesh):
    return jax.shard_map(
        shards,
        mesh=mesh,
        in_specs=(
            P("dp", "tensor", None),
            P("dp", "tensor", None),
            P("dp", "tensor"),
            P("dp", None, "tensor"),
            P("dp", None, "tensor"),
            P("dp", None, "tensor"),
            P("dp", "tensor"),
            P("dp", "tensor"),
            P("dp", "tensor"),
            P("dp", None),
            P("dp", None),
            P("dp", None),
            P("dp", "tensor"),
            P("dp", "tensor"),
            P("dp", "tensor"),
            P(None, "tensor"),
            P(None, "tensor"),
            P(None, "tensor"),
            P(None, "tensor"),
            P(None, "tensor"),
            P(None, "tensor"),
            P(),
            P(),
            P(),
            P(),
            P(),
            P(),
        ),
        out_specs=(
            P("dp", "tensor", None),
            P("dp", "tensor", None),
            P("dp", None, "tensor"),
            P("dp", None, "tensor"),
            P("dp", None, "tensor"),
            P("dp", "tensor"),
            P("dp", "tensor"),
            P("dp", "tensor"),
            P("dp", None),
            P("dp", None),
            P("dp", None),
            P("dp", "tensor"),
            P("dp", "tensor"),
            P("dp", "tensor"),
            P(None, "tensor"),
            P(None, "tensor"),
            P(None, "tensor"),
            P(None, "tensor"),
            P(None, "tensor"),
            P(None, "tensor"),
            P(),
            P(),
            P(),
            P(),
            P(),
            P(),
        ),
        check_vma=False,
    )
```

profile of v0, /device:TPU:0, one launch (start us, length us, event | category | flops | bytes accessed | tf_op | source)
XLA Modules:
  0.0 1990.6 jit_solution(14885463930269182497)
XLA Ops:
  24.1 26.9 %all-gather = bf16[8,96,6]{1,2,0:T(8,128)(2,1)S(1)} all-gather(bf16[1,96,6]{1,2,0:T(8,128)(2,1)S(1)} %convert_bitcast_fusion), channel_id=1, replica_groups=mesh['dp'=8,'tensor'=4] {'dp'}, dimensions={0}, use_global_device_ids=true | all-gather | bytes 10368 | tf_op jit(solution)/shard_map/all_gather | solution.py:193
  51.1 33.1 %all_gather.25 = bf16[768,256]{1,0:T(8,128)(2,1)} all-gather(bf16[96,256]{1,0:T(8,128)(2,1)S(1)} %convert_element_type.75), channel_id=1, replica_groups=mesh['dp'=8,'tensor'=4] {'dp'}, dimensions={0}, use_global_device_ids=true | all-gather | bytes 442368 | tf_op jit(solution)/shard_map/all_gather | solution.py:194
  86.3 15.7 all-gather.5.cloned.1.call-done
  122.4 15.2 multiply_convert_fusion.1
  167.6 430.2 %while.97 = (s32[]{:T(128)}, f32[6,64,128]{2,1,0:T(8,128)S(1)}, s32[]{:T(128)}, f32[16,256,6,64]{1,0,3,2:T(8,128)}, f32[16,6,64,128]{3,2,1,0:T(8,128)}, /*index=...) while((s32[]{:T(128)}, f32[6,64,128]{2,1,0:T(8,128)S(1)}, ...), condition=%wide.region_4.5_spmd.clone, body=%wide.region_1.4_spmd.clone.sunk | while | flops 707747840 | bytes 6289401 | solution.py:97
  184.0 9.9 dynamic_update_slice.118
  210.9 9.9 dynamic_update_slice.118
  237.8 9.9 dynamic_update_slice.118
  264.7 9.9 dynamic_update_slice.118
  291.6 9.9 dynamic_update_slice.118
  318.5 9.9 dynamic_update_slice.118
  345.4 9.9 dynamic_update_slice.118
  372.3 9.9 dynamic_update_slice.118
  399.2 9.9 dynamic_update_slice.118
  479.7 9.9 dynamic_update_slice.118
  506.6 9.9 dynamic_update_slice.118
  533.4 9.9 dynamic_update_slice.118
  560.3 9.9 dynamic_update_slice.118
  587.2 9.9 dynamic_update_slice.118
  597.8 11.4 copy.348
  623.4 10.3 psum.49
  643.4 64.4 %reduce-scatter.21.cloned.1.call-done = f32[96,384]{1,0:T(8,128)} async-done(((f32[768,384]{1,0:T(8,128)}), f32[96,384]{1,0:T(8,128)}) %reduce-scatter.21.cloned.1.call-update) | async-done | bytes 147472 | tf_op jit(solution)/shard_map/reduce_scatter | solution.py:280
  709.6 31.6 %all_gather.26 = bf16[768,384]{1,0:T(8,128)(2,1)S(1)} all-gather(bf16[96,384]{1,0:T(8,128)(2,1)S(1)} %get-tuple-element.1313), channel_id=1, replica_groups=mesh['dp'=8,'tensor'=4] {'dp'}, dimensions={0}, use_global_device_ids=true | all-gather | bytes 663552 | tf_op jit(solution)/shard_map/all_gather | solution.py:195
  750.5 10.1 psum.50
  760.6 14.0 fusion.152
  795.9 649.0 %while.98 = (s32[]{:T(128)}, f32[6]{0:T(128)S(1)}, f32[6]{0:T(128)S(1)}, f32[6,64,128]{2,1,0:T(8,128)S(1)}, f32[16,256,6,64]{1,0,3,2:T(8,128)}, /*index=5*/f32[1...) while((s32[]{:T(128)}, f32[6]{0:T(128)S(1)}, ...), condition=%wide.region_24.25_spmd.clone, body=%wide.region_10.24_spmd.clone.sunk | while | flops 1670961152 | bytes 15330028 | solution.py:97
  822.9 9.9 dynamic_update_slice.123
  863.4 9.9 dynamic_update_slice.123
  944.5 9.9 dynamic_update_slice.123
  1147.0 9.9 dynamic_update_slice.123
  1187.6 9.9 dynamic_update_slice.123
  1228.2 9.9 dynamic_update_slice.123
  1268.7 9.9 dynamic_update_slice.123
  1309.3 9.9 dynamic_update_slice.123
  1349.8 9.9 dynamic_update_slice.123
  1390.4 9.9 dynamic_update_slice.123
  1430.9 9.9 dynamic_update_slice.123
  1458.7 16.6 multiply_reduce_fusion.9
  1487.5 10.3 fusion.101
  1517.6 54.0 %all-reduce.37.cloned.1.call-done = f32[1,4096,256]{2,1,0:T(8,128)} async-done(((f32[1,4096,256]{2,1,0:T(8,128)}), f32[1,4096,256]{2,1,0:T(8,128)}) %all-reduce.37.cloned.1.call-update) | async-done | bytes 4194320 | tf_op jit(solution)/shard_map/psum | solution.py:250
  1571.6 11.9 multiply_reduce_fusion.15
  1591.3 11.9 fusion.107
  1618.1 10.8 convolution_bitcast_fusion.2
  1638.2 63.7 %reduce-scatter.17.cloned.1.call-done = f32[96,256]{1,0:T(8,128)} async-done(((f32[768,256]{1,0:T(8,128)}), f32[96,256]{1,0:T(8,128)}) %reduce-scatter.17.cloned.1.call-update) | async-done | bytes 98320 | tf_op jit(solution)/shard_map/reduce_scatter | solution.py:279
  1703.6 70.3 %reduce-scatter.15.cloned.1.call-done = f32[96,2,384]{2,0,1:T(8,128)} async-done(((f32[768,2,384]{2,0,1:T(8,128)}), f32[96,2,384]{2,0,1:T(8,128)}) %reduce-scatter.15.cloned.1.call-update) | async-done | bytes 294928 | tf_op jit(solution)/shard_map/reduce_scatter | solution.py:277
  1778.0 96.6 %reduce-scatter.13.cloned.1.call-done = f32[1,1024,768]{2,1,0:T(8,128)} async-done(((f32[1,4096,768]{2,1,0:T(8,128)}), f32[1,1024,768]{2,1,0:T(8,128)}) %reduce-scatter.13.cloned.1.call-update) | async-done | bytes 3145744 | tf_op jit(solution)/shard_map/reduce_scatter | solution.py:263
  1880.0 40.3 %all-reduce.34 = (f32[6,1536]{1,0:T(8,128)S(1)}, f32[3,24]{1,0:T(4,128)S(1)}, f32[5,256]{1,0:T(8,128)S(1)}, f32[768]{0:T(1024)S(1)}) all-reduce(f32[6,1536]{1,0:T(8,128)} %copy-done.23, f32[3,24]{1,0:T(4,128)} %copy-done.63, f32[5,256]{1,0:T(8,128)S(1)} %add_multiply_fusion, ...), channel_id=1, replica_groups=mesh['dp'=8,'tensor'=4] {'dp','tensor'}, use_global_device_ids=true, to_apply=%region_38.39 | all-reduce | flops 11336 | bytes 90688 | tf_op jit(solution)/shard_map/psum | solution.py:294
  1926.4 50.4 %reduce-scatter.11.cloned.1.call-done = f32[1,1024,768]{2,1,0:T(8,128)} async-done(((f32[1,4096,768]{2,1,0:T(8,128)}), f32[1,1024,768]{2,1,0:T(8,128)}) %reduce-scatter.11.cloned.1.call-update) | async-done | bytes 3145744 | tf_op jit(solution)/shard_map/reduce_scatter | solution.py:236
  (1569 shorter events, 1011.0 us)
Async XLA Ops:
  7.2 14.5 copy-start.34
  7.2 77.6 %all-gather.7.cloned.1.call-start = ((), (), s32[]{:S(2)}) async-start(), calls=%async_computation.7 | async-start | bytes 1327104 | tf_op jit(solution)/shard_map/all_gather | solution.py:192
  9.0 14.5 copy-start.64
  9.0 15.1 copy-start.48
  9.0 42.1 %copy-start.20 = (f32[96,256]{1,0:T(8,128)S(1)}, f32[96,256]{1,0:T(8,128)}, u32[]{:S(2)}) copy-start(f32[96,256]{1,0:T(8,128)} %param.40) | copy-start | bytes 294916
  9.0 75.2 %copy-start.37 = (f32[5,256]{1,0:T(8,128)S(1)}, f32[5,256]{1,0:T(8,128)}, u32[]{:S(2)}) copy-start(f32[5,256]{1,0:T(8,128)} %param.52) | copy-start | bytes 15364
  9.0 92.9 %all-gather.5.cloned.1.call-start = ((), (), s32[]{:S(2)}) async-start(), calls=%async_computation.6 | async-start | bytes 7864320 | tf_op jit(solution)/shard_map/all_gather | solution.py:205
  14.5 619.2 %all-gather.9.cloned.1.call-start = ((), (), s32[]{:S(2)}) async-start(), calls=%async_computation.9 | async-start | bytes 7864320 | tf_op jit(solution)/shard_map/all_gather | solution.py:238
  15.2 692.6 %reduce-scatter.21.cloned.1.call-start = ((), (), s32[]{:S(2)}) async-start(), calls=%async_computation.15 | async-start | bytes 1327104 | tf_op jit(solution)/shard_map/reduce_scatter | solution.py:280
  51.1 66.9 %copy-start.27 = (bf16[768,6]{0,1:T(8,128)(2,1)}, bf16[768,6]{0,1:T(8,128)(2,1)S(1)}, u32[]{:S(2)}) copy-start(bf16[768,6]{0,1:T(8,128)(2,1)S(1)} %reshape.757) | copy-start | bytes 27652
  86.3 23.1 %copy-start.15 = (bf16[96,8,2,384]{3,1,2,0:T(8,128)(2,1)}, bf16[96,8,2,384]{3,1,2,0:T(8,128)(2,1)S(1)}, u32[]{:S(2)}) copy-start(bf16[96,8,2,384]{3,1,2,0:T(8,128)(2,1)S(1)} %copy.346) | copy-start | bytes 3538948
  141.8 12.1 slice-start
  615.8 18.0 copy-start.35
  633.7 74.1 %copy-start.24 = (f32[96,384]{1,0:T(8,128)S(1)}, f32[96,384]{1,0:T(8,128)}, u32[]{:S(2)}) copy-start(f32[96,384]{1,0:T(8,128)} %param.43) | copy-start | bytes 442372
  633.8 74.1 %copy-start.25 = (f32[96,384]{1,0:T(8,128)S(1)}, f32[96,384]{1,0:T(8,128)}, u32[]{:S(2)}) copy-start(f32[96,384]{1,0:T(8,128)} %param.45) | copy-start | bytes 442372
  633.8 74.1 %copy-start.26 = (f32[96,384]{1,0:T(8,128)S(1)}, f32[96,384]{1,0:T(8,128)}, u32[]{:S(2)}) copy-start(f32[96,384]{1,0:T(8,128)} %param.44) | copy-start | bytes 442372
  642.6 929.0 %all-reduce.37.cloned.1.call-start = ((), (), s32[]{:S(2)}) async-start(), calls=%async_computation.11 | async-start | bytes 8388608 | tf_op jit(solution)/shard_map/psum | solution.py:250
  741.2 9.4 copy-start.13
  1458.7 16.6 copy-start.42
  1458.7 16.6 copy-start.44
  1458.7 16.6 copy-start.45
  1475.3 9.3 copy-start.3
  1475.3 9.3 copy-start.8
  1475.3 9.3 copy-start.9
  1486.8 149.8 %reduce-scatter.19.cloned.1.call-start = ((), (), s32[]{:S(2)}) async-start(), calls=%async_computation.14 | async-start | bytes 442368
  1487.5 11.9 copy-start.5
  1517.6 184.3 %reduce-scatter.17.cloned.1.call-start = ((), (), s32[]{:S(2)}) async-start(), calls=%async_computation.13 | async-start | bytes 884736 | tf_op jit(solution)/shard_map/reduce_scatter | solution.py:279
  1571.6 12.0 copy-start.55
  1571.6 12.0 copy-start.57
  1571.6 12.0 copy-start.59
  1591.2 182.6 %reduce-scatter.15.cloned.1.call-start = ((), (), s32[]{:S(2)}) async-start(), calls=%async_computation.12 | async-start | bytes 2654208 | tf_op jit(solution)/shard_map/reduce_scatter | solution.py:277
  1603.3 271.3 %reduce-scatter.13.cloned.1.call-start = ((), (), s32[]{:S(2)}) async-start(), calls=%async_computation.10 | async-start | bytes 15728640 | tf_op jit(solution)/shard_map/reduce_scatter | solution.py:263
  1617.0 359.8 %reduce-scatter.11.cloned.1.call-start = ((), (), s32[]{:S(2)}) async-start(), calls=%async_computation.8 | async-start | bytes 15728640 | tf_op jit(solution)/shard_map/reduce_scatter | solution.py:236
  1629.0 9.1 copy-start.67
  1629.0 9.1 copy-start.68
  1629.0 9.1 copy-start.65
  1629.1 72.9 %copy-start.21 = (f32[96,256]{1,0:T(8,128)S(1)}, f32[96,256]{1,0:T(8,128)}, u32[]{:S(2)}) copy-start(f32[96,256]{1,0:T(8,128)} %param.40) | copy-start | bytes 294916
  1629.1 72.8 %copy-start.29 = (f32[96,256]{1,0:T(8,128)S(1)}, f32[96,256]{1,0:T(8,128)}, u32[]{:S(2)}) copy-start(f32[96,256]{1,0:T(8,128)} %param.42) | copy-start | bytes 294916
  1629.1 72.8 %copy-start.30 = (f32[96,256]{1,0:T(8,128)S(1)}, f32[96,256]{1,0:T(8,128)}, u32[]{:S(2)}) copy-start(f32[96,256]{1,0:T(8,128)} %param.41) | copy-start | bytes 294916
  1629.1 144.7 %copy-start.16 = (f32[96,2,384]{2,1,0:T(2,128)S(1)}, f32[96,2,384]{2,1,0:T(2,128)}, u32[]{:S(2)}) copy-start(f32[96,2,384]{2,1,0:T(2,128)} %param.34) | copy-start | bytes 884740
  1629.1 144.7 %copy-start.22 = (f32[96,2,384]{2,1,0:T(2,128)S(1)}, f32[96,2,384]{2,1,0:T(2,128)}, u32[]{:S(2)}) copy-start(f32[96,2,384]{2,1,0:T(2,128)} %param.36) | copy-start | bytes 884740
  1629.1 245.4 %copy-start.4 = (bf16[1,1024,768]{2,1,0:T(8,128)(2,1)S(1)}, bf16[1,1024,768]{2,1,0:T(8,128)(2,1)}, u32[]{:S(2)}) copy-start(bf16[1,1024,768]{2,1,0:T(8,128)(2,1)} %param.31) | copy-start | bytes 4718596
  1629.2 245.4 %copy-start.12 = (bf16[768,256]{1,0:T(8,128)(2,1)S(1)}, bf16[768,256]{1,0:T(8,128)(2,1)}, u32[]{:S(2)}) copy-start(bf16[768,256]{1,0:T(8,128)(2,1)} %all_gather.25) | copy-start | bytes 1179652
  1629.2 245.4 %copy-start.31 = (f32[768]{0:T(1024)S(1)}, f32[768]{0:T(1024)}, u32[]{:S(2)}) copy-start(f32[768]{0:T(1024)} %param.55) | copy-start | bytes 9220
  1629.2 245.4 %copy-start.33 = (f32[1024]{0:T(1024)S(1)}, f32[1024]{0:T(1024)}, u32[]{:S(2)}) copy-start(f32[1024]{0:T(1024)} %copy-done.32) | copy-start | bytes 12292
  1631.0 146.0 %copy-start.63 = (f32[3,24]{1,0:T(4,128)}, f32[3,24]{1,0:T(4,128)S(1)}, u32[]{:S(2)}) copy-start(f32[3,24]{1,0:T(4,128)S(1)} %dynamic_update_slice.97) | copy-start | bytes 868
  1631.1 146.0 %copy-start.23 = (f32[6,1536]{1,0:T(8,128)}, f32[6,1536]{1,0:T(8,128)S(1)}, u32[]{:S(2)}) copy-start(f32[6,1536]{1,0:T(8,128)S(1)} %maximum_dynamic-update-slice_fusion) | copy-start | bytes 110596
  1778.0 198.9 %copy-start.10 = (bf16[1,1024,768]{2,1,0:T(8,128)(2,1)S(1)}, bf16[1,1024,768]{2,1,0:T(8,128)(2,1)}, u32[]{:S(2)}) copy-start(bf16[1,1024,768]{2,1,0:T(8,128)(2,1)} %param.32) | copy-start | bytes 4718596
  (44 other events, 193.8 us)
Sparse Core Ops, SparseCore 0:
  10.8 43.9 all-gather.6
  57.0 44.9 all-gather.4
  103.6 46.3 all-gather.8
  642.7 65.0 reduce-scatter.20
  1486.9 84.6 all-reduce.36
  1575.1 61.4 reduce-scatter.18
  1640.3 61.5 reduce-scatter.16
  1706.0 67.8 reduce-scatter.14
  1776.4 98.1 reduce-scatter.12
  1877.0 99.7 reduce-scatter.10
where the time goes:
time: 2010 us; the launch traced here: 1990 us
  local copies, waits for them, and re-layouts  590 us (29%)
  waiting for transfers between devices  422 us (21%)
  other arithmetic  403 us (20%)
  matrix products  355 us (18%)
  blocking collectives  158 us (8%)
  loops' own time  46.8 us (2%)
    dynamic_update_slice x80, local copies, waits for them, and re-layouts, scan_states(): lax.scan(step_fn, start, (split_blocks(inputs_x), split_blocks(inputs_b),...  331 us
    another operation x114, other arithmetic  182 us
    dot_general x48, matrix products, span_step(): inner_part = jnp.einsum('hts,shp->thp', weights, block_x, precision=HIGHEST)  112 us
    reduce_scatter x1, waiting for transfers between devices, shards(): lax.psum_scatter(summed_grads.reshape(sequence_count, length, model_width...  96.6 us
    reduce_scatter x1, waiting for transfers between devices, shards(): lax.psum_scatter(inner_grad, 'dp', scatter_dimension=0, tiled=True)  70.3 us
    dot_general x64, matrix products, span_step(): scores = jnp.dot(block_c, block_b.T, precision=HIGHEST)  64.5 us
    reduce_scatter x1, waiting for transfers between devices, shards(): lax.psum_scatter(outer_grad, 'dp', scatter_dimension=0, tiled=True)  64.4 us
    reduce_scatter x1, waiting for transfers between devices, shards(): lax.psum_scatter(state_grad, 'dp', scatter_dimension=0, tiled=True)  63.7 us
  transfers between devices with their start and end apart: 10, of which 8 were waited for; matrix products, arithmetic and copies ran while one was open for 30% of the time, Pallas kernels for 0%

commit v1 on v0

--- a/solution.py
+++ b/solution.py
@@ -3,6 +3,8 @@
 import jax
 import jax.numpy as jnp
 from jax import lax
+from jax.experimental import pallas as pl
+from jax.experimental.pallas import tpu as pltpu
 from jax.sharding import PartitionSpec as P
 
 SPAN = 256
@@ -48,64 +50,271 @@
     return filtered
 
 
-def span_step(rates, skip, carry, pieces):
-    carry_state, last_seg = carry
-    block_x, block_b, block_c, block_dt, block_seg = pieces
-    block_rows = block_seg.shape[0]
-    log_decay = jnp.cumsum(block_dt * rates, axis=0)
-    positions = jnp.arange(block_rows)
-    same_doc = (block_seg[:, None] == block_seg[None, :]) & (
-        positions[:, None] >= positions[None, :]
-    )
-    log_gaps = log_decay.T[:, :, None] - log_decay.T[:, None, :]
-    decays = jnp.where(same_doc[None], jnp.exp(jnp.where(same_doc[None], log_gaps, 0.0)), 0.0)
-    scores = jnp.dot(block_c, block_b.T, precision=HIGHEST)
-    weights = decays * scores[None] * block_dt.T[:, None, :]
-    inner_part = jnp.einsum("hts,shp->thp", weights, block_x, precision=HIGHEST)
-    carried = jnp.where((block_seg == last_seg)[:, None], jnp.exp(log_decay), 0.0)
-    outer_part = (
-        jnp.einsum("hpn,tn->thp", carry_state, block_c, precision=HIGHEST) * carried[:, :, None]
-    )
-    end_seg = block_seg[block_rows - 1]
-    tail_weight = (
-        jnp.where(
-            (block_seg == end_seg)[:, None],
-            jnp.exp(log_decay[block_rows - 1][None, :] - log_decay),
-            0.0,
+def exact_dot(left, right):
+    return jnp.dot(left, right, precision=HIGHEST, preferred_element_type=jnp.float32)
+
+
+def rows_dot(left, right, precision=None):
+    return lax.dot_general(
+        left,
+        right,
+        (((0,), (0,)), ((), ())),
+        precision=precision,
+        preferred_element_type=jnp.float32,
+    )
+
+
+def lanes_dot(left, right):
+    return lax.dot_general(
+        left, right, (((1,), (1,)), ((), ())), preferred_element_type=jnp.float32
+    )
+
+
+def two_parts(value):
+    high = value.astype(jnp.bfloat16)
+    return high, (value - high.astype(jnp.float32)).astype(jnp.bfloat16)
+
+
+def softplus(value):
+    return jnp.maximum(value, 0.0) + jnp.log(1.0 + jnp.exp(-jnp.abs(value)))
+
+
+def block_terms(heads, width, step_ref, marks_ref, seg_ref, head_ref):
+    span = step_ref.shape[1]
+    pre = step_ref[0] + head_ref[0:1, :]
+    dt = softplus(pre)
+    rates = -jnp.exp(head_ref[1:2, :])
+    row = lax.broadcasted_iota(jnp.int32, (span, span), 0)
+    col = lax.broadcasted_iota(jnp.int32, (span, span), 1)
+    lower = jnp.where(row >= col, 1.0, 0.0).astype(jnp.float32)
+    upper = jnp.where(row <= col, 1.0, 0.0).astype(jnp.float32)
+    eye = jnp.where(row == col, 1.0, 0.0).astype(jnp.float32)
+    scaled = dt * rates
+    lam = exact_dot(lower, scaled)
+    lam_row = rows_dot(scaled, upper, HIGHEST)
+    dt_row = rows_dot(dt, eye, HIGHEST)
+    marks = marks_ref[0]
+    mask = (marks[:, 0:1] == seg_ref[0, 0]) & (row >= col)
+    carried = marks[:, 1:2] * jnp.exp(lam)
+    tail = marks[:, 2:3] * jnp.exp(lam[span - 1 : span, :] - lam) * dt
+    lane = lax.broadcasted_iota(jnp.int32, (heads, heads * width), 1) // width
+    head = lax.broadcasted_iota(jnp.int32, (heads, heads * width), 0)
+    spread = jnp.where(lane == head, 1.0, 0.0).astype(jnp.float32)
+    return pre, dt, rates, lam, lam_row, dt_row, mask, carried, tail, spread, upper
+
+
+def decay_weights(lam, lam_row, dt_row, mask, h):
+    gaps = jnp.where(mask, lam[:, h : h + 1] - lam_row[h : h + 1, :], -1e30)
+    return jnp.exp(gaps) * dt_row[h : h + 1, :]
+
+
+def scan_kernel(
+    heads, width, x_ref, bc_ref, step_ref, marks_ref, seg_ref, head_ref, y_ref, save_ref, state
+):
+    n = bc_ref.shape[2] // 2
+
+    @pl.when(pl.program_id(1) == 0)
+    def _():
+        state[...] = jnp.zeros_like(state)
+
+    pre, dt, rates, lam, lam_row, dt_row, mask, carried, tail, spread, upper = block_terms(
+        heads, width, step_ref, marks_ref, seg_ref, head_ref
+    )
+    b = bc_ref[0, :, :n]
+    c = bc_ref[0, :, n:]
+    scores = lanes_dot(c, b)
+    old = state[...]
+    save_ref[0, 0] = old
+    x = x_ref[0].astype(jnp.float32)
+    skip = exact_dot(head_ref[2:3, :], spread)
+    span = x.shape[0]
+    old_high, old_low = two_parts(old)
+    rest = (matmul(c, old_high) + matmul(c, old_low)) * exact_dot(carried, spread) + skip * x
+    pair = 2 * width
+    side = lax.broadcasted_iota(jnp.int32, (span, pair), 1) < width
+    for p in range(heads // 2):
+        at = slice(p * pair, (p + 1) * pair)
+        xp = x[:, at]
+        left = jnp.where(side, xp, 0.0).astype(jnp.bfloat16)
+        right = jnp.where(side, 0.0, xp).astype(jnp.bfloat16)
+        high0, low0 = two_parts(decay_weights(lam, lam_row, dt_row, mask, 2 * p) * scores)
+        high1, low1 = two_parts(decay_weights(lam, lam_row, dt_row, mask, 2 * p + 1) * scores)
+        y_ref[0, :, at] = (
+            (matmul(high0, left) + matmul(low0, left))
+            + (matmul(high1, right) + matmul(low1, right))
+            + rest[:, at]
         )
-        * block_dt
-    )
-    kept = jnp.where(last_seg == end_seg, jnp.exp(log_decay[block_rows - 1]), 0.0)
-    fresh_state = jnp.einsum("th,thp,tn->hpn", tail_weight, block_x, block_b, precision=HIGHEST)
-    new_state = carry_state * kept[:, None, None] + fresh_state
-    result = inner_part + outer_part + skip[None, :, None] * block_x
-    return ((new_state, end_seg), result)
-
-
-def scan_states(inputs_x, inputs_b, inputs_c, step_sizes, segment, rates, skip):
-    seq_len = inputs_x.shape[0]
-    blocks = seq_len // SPAN
-
-    def split_blocks(values):
-        return values.reshape((blocks, SPAN) + values.shape[1:])
-
-    start = (
-        jnp.zeros((inputs_x.shape[1], inputs_x.shape[2], inputs_b.shape[1]), jnp.float32),
-        jnp.array(-1, jnp.int32),
-    )
-    step_fn = jax.checkpoint(partial(span_step, rates, skip))
-    final, outputs = lax.scan(
-        step_fn,
-        start,
-        (
-            split_blocks(inputs_x),
-            split_blocks(inputs_b),
-            split_blocks(inputs_c),
-            split_blocks(step_sizes),
-            split_blocks(segment),
-        ),
-    )
-    return outputs.reshape(inputs_x.shape)
+    kept = exact_dot(carried[span - 1 : span, :], spread)
+    tail_high, tail_low = two_parts(x * exact_dot(tail, spread))
+    state[...] = old * kept + (rows_dot(b, tail_high) + rows_dot(b, tail_low))
+
+
+def back_kernel(
+    heads,
+    width,
+    x_ref,
+    bc_ref,
+    step_ref,
+    marks_ref,
+    seg_ref,
+    head_ref,
+    y_ref,
+    dy_ref,
+    save_ref,
+    dx_ref,
+    dbc_ref,
+    dstep_ref,
+    skip_ref,
+    small_ref,
+    grad,
+):
+    n = bc_ref.shape[2] // 2
+
+    @pl.when(pl.program_id(1) == 0)
+    def _():
+        grad[...] = jnp.zeros_like(grad)
+        skip_ref[...] = jnp.zeros_like(skip_ref)
+        small_ref[...] = jnp.zeros_like(small_ref)
+
+    pre, dt, rates, lam, lam_row, dt_row, mask, carried, tail, spread, upper = block_terms(
+        heads, width, step_ref, marks_ref, seg_ref, head_ref
+    )
+    b = bc_ref[0, :, :n]
+    c = bc_ref[0, :, n:]
+    scores = lanes_dot(c, b)
+    x = x_ref[0].astype(jnp.float32)
+    dy = dy_ref[0]
+    skip = exact_dot(head_ref[2:3, :], spread)
+    span = x.shape[0]
+    old = save_ref[0, 0]
+    later = grad[...]
+    later_high, later_low = two_parts(later)
+    tail_wide = exact_dot(tail, spread)
+    carried_wide = exact_dot(carried, spread)
+    tail_x = tail_wide * x
+    carried_high, carried_low = two_parts(carried_wide * dy)
+    from_state = matmul(b, later_high) + matmul(b, later_low)
+    pair = 2 * width
+    side = lax.broadcasted_iota(jnp.int32, (span, pair), 1) < width
+    total = jnp.zeros((span, span), jnp.float32)
+    pulled = []
+    for p in range(heads // 2):
+        at = slice(p * pair, (p + 1) * pair)
+        dyp = dy[:, at]
+        xp = x_ref[0, :, at]
+        left = jnp.concatenate(two_parts(jnp.where(side, dyp, 0.0)), 1)
+        right = jnp.concatenate(two_parts(jnp.where(side, 0.0, dyp)), 1)
+        twice = jnp.concatenate([xp, xp], 1)
+        d0 = decay_weights(lam, lam_row, dt_row, mask, 2 * p)
+        d1 = decay_weights(lam, lam_row, dt_row, mask, 2 * p + 1)
+        total = total + d0 * lanes_dot(left, twice) + d1 * lanes_dot(right, twice)
+        high0, low0 = two_parts(d0 * scores)
+        high1, low1 = two_parts(d1 * scores)
+        both = (rows_dot(high0, left) + rows_dot(low0, left)) + (
+            rows_dot(high1, right) + rows_dot(low1, right)
+        )
+        pulled.append(both[:, :pair] + both[:, pair:])
+    inner = jnp.concatenate(pulled, 1)
+    dx_ref[0] = inner + tail_wide * from_state + skip * dy
+    total = total.astype(jnp.bfloat16)
+    dbc_ref[0, :, :n] = rows_dot(total, c) + lanes_dot(tail_x.astype(jnp.bfloat16), later_high)
+    dbc_ref[0, :, n:] = jnp.dot(total, b, preferred_element_type=jnp.float32) + lanes_dot(
+        carried_high, old.astype(jnp.bfloat16)
+    )
+    gather = spread.T
+    tail_part = exact_dot(tail_x * from_state, gather)
+    columns = exact_dot(inner * x, gather) + tail_part
+    rows = exact_dot(dy * (y_ref[0] - skip * x), gather)
+    kept = carried[span - 1 : span, :]
+    kept_wide = exact_dot(kept, spread)
+    across = exact_dot(jnp.sum(later * old, axis=0, keepdims=True) * kept_wide, gather)
+    end = across + jnp.sum(tail_part, axis=0, keepdims=True)
+    lam_grad = exact_dot(upper, rows - columns) + end
+    dt_grad = lam_grad * rates + columns / jnp.maximum(dt, 1e-30)
+    dstep = dt_grad / (1.0 + jnp.exp(-pre))
+    dstep_ref[0] = dstep
+    skip_ref[0, 0:1, :] += jnp.sum(x * dy, axis=0, keepdims=True)
+    small_ref[0, 0:1, :] += jnp.sum(dstep, axis=0, keepdims=True)
+    small_ref[0, 1:2, :] += jnp.sum(dt * lam_grad, axis=0, keepdims=True) * rates
+    grad[...] = later * kept_wide + (rows_dot(c, carried_high) + rows_dot(c, carried_low))
+
+
+def scan_specs(blocks, back, heads, inner, states):
+    def place(i):
+        return blocks - 1 - i if back else i
+
+    return [
+        pl.BlockSpec((1, SPAN, inner), lambda s, i: (s, place(i), 0)),
+        pl.BlockSpec((1, SPAN, states), lambda s, i: (s, place(i), 0)),
+        pl.BlockSpec((1, SPAN, heads), lambda s, i: (s, place(i), 0)),
+        pl.BlockSpec((1, SPAN, 8), lambda s, i: (s, place(i), 0)),
+        pl.BlockSpec((1, 1, 1, SPAN), lambda s, i: (s, place(i), 0, 0)),
+        pl.BlockSpec((3, heads), lambda s, i: (0, 0)),
+    ], pl.BlockSpec((1, 1, states // 2, inner), lambda s, i: (s, place(i), 0, 0))
+
+
+PARAMS = pltpu.CompilerParams(
+    vmem_limit_bytes=48 * 1024 * 1024, dimension_semantics=("arbitrary", "arbitrary")
+)
+
+
+def scan_forward(x, bc, step_raw, marks, seg_rows, head_vec):
+    count, length, inner = x.shape
+    heads, states, blocks = head_vec.shape[1], bc.shape[2], x.shape[1] // SPAN
+    specs, save = scan_specs(blocks, False, heads, inner, states)
+    return pl.pallas_call(
+        partial(scan_kernel, heads, inner // heads),
+        grid=(count, blocks),
+        in_specs=specs,
+        out_specs=[specs[0], save],
+        out_shape=[
+            jax.ShapeDtypeStruct((count, length, inner), jnp.float32),
+            jax.ShapeDtypeStruct((count, blocks, states // 2, inner), jnp.float32),
+        ],
+        scratch_shapes=[pltpu.VMEM((states // 2, inner), jnp.float32)],
+        compiler_params=PARAMS,
+        name="scan_forward",
+    )(x, bc, step_raw, marks, seg_rows, head_vec)
+
+
+def scan_backward(x, bc, step_raw, marks, seg_rows, head_vec, y, dy, saved):
+    count, length, inner = x.shape
+    heads, states, blocks = head_vec.shape[1], bc.shape[2], x.shape[1] // SPAN
+    specs, save = scan_specs(blocks, True, heads, inner, states)
+    return pl.pallas_call(
+        partial(back_kernel, heads, inner // heads),
+        grid=(count, blocks),
+        in_specs=specs + [specs[0], specs[0], save],
+        out_specs=[
+            specs[0],
+            specs[1],
+            specs[2],
+            pl.BlockSpec((1, 8, inner), lambda s, i: (s, 0, 0)),
+            pl.BlockSpec((1, 8, heads), lambda s, i: (s, 0, 0)),
+        ],
+        out_shape=[
+            jax.ShapeDtypeStruct((count, length, inner), jnp.float32),
+            jax.ShapeDtypeStruct((count, length, states), jnp.float32),
+            jax.ShapeDtypeStruct((count, length, heads), jnp.float32),
+            jax.ShapeDtypeStruct((count, 8, inner), jnp.float32),
+            jax.ShapeDtypeStruct((count, 8, heads), jnp.float32),
+        ],
+        scratch_shapes=[pltpu.VMEM((states // 2, inner), jnp.float32)],
+        compiler_params=PARAMS,
+        name="scan_backward",
+    )(x, bc, step_raw, marks, seg_rows, head_vec, y, dy, saved)
+
+
+def segment_marks(segment):
+    count, length = segment.shape
+    blocks = length // SPAN
+    by_block = segment.reshape(count, blocks, SPAN)
+    ends = by_block[:, :, SPAN - 1 :]
+    before = jnp.pad(ends, ((0, 0), (1, 0), (0, 0)), constant_values=-1)[:, :blocks]
+    columns = [by_block, by_block == before, by_block == ends]
+    stacked = jnp.stack([v.astype(jnp.float32) for v in columns], -1)
+    marks = jnp.pad(stacked, ((0, 0), (0, 0), (0, 0), (0, 5))).reshape(count, length, 8)
+    return marks, by_block[:, :, None, :].astype(jnp.float32)
 
 
 def filter_parts(segment, inner_raw, state_raw, channel_taps, state_taps):
@@ -117,31 +326,6 @@
         causal_filter(state_raw, state_taps[:taps_count], state_taps[taps_count], segment)
     )
     return (active_inner, active_state)
-
-
-def mixer_part(segment, active_inner, active_state, step_raw, gate_raw, head_vec):
-    sequence_count, length, local_inner = active_inner.shape
-    heads_here = head_vec.shape[1]
-    state_width = active_state.shape[2] // 2
-    step_sizes = jax.nn.softplus(step_raw + head_vec[0])
-    rates = -jnp.exp(head_vec[1])
-    split_inner = active_inner.reshape(
-        sequence_count, length, heads_here, local_inner // heads_here
-    )
-
-    def one_sequence(pieces):
-        return scan_states(
-            pieces[0],
-            pieces[1][:, :state_width],
-            pieces[1][:, state_width:],
-            pieces[2],
-            pieces[3],
-            rates,
-            head_vec[2],
-        )
-
-    mixed_heads = lax.map(one_sequence, (split_inner, active_state, step_sizes, segment))
-    return mixed_heads.reshape(active_inner.shape) * jax.nn.silu(gate_raw)
 
 
 def adam_update(weight, gradient, moment_one, moment_two, step_rate, decay_rate):
@@ -188,15 +372,28 @@
     tensor_size = lax.axis_size("tensor")
     tensor_rank = lax.axis_index("tensor")
     taps_count = state_filter.shape[0] - 1
-    inner_weight, step_weight, state_weight, outer_weight = (
-        lax.all_gather(inner_proj.astype(jnp.bfloat16), "dp", axis=0, tiled=True),
-        lax.all_gather(step_proj.astype(jnp.bfloat16), "dp", axis=0, tiled=True),
-        lax.all_gather(state_proj.astype(jnp.bfloat16), "dp", axis=0, tiled=True),
-        lax.all_gather(outer_proj.astype(jnp.bfloat16), "dp", axis=0, tiled=True),
-    )
-    local_inner = inner_weight.shape[2]
-    heads_here = step_weight.shape[1]
-    state_cols = state_weight.shape[1]
+    local_inner = inner_proj.shape[2]
+    heads_here = step_proj.shape[1]
+    state_cols = state_proj.shape[1]
+    all_cols = lax.all_gather(
+        jnp.concatenate(
+            [
+                inner_proj.reshape(-1, 2 * local_inner),
+                state_proj,
+                outer_proj,
+                step_proj,
+            ],
+            1,
+        ).astype(jnp.bfloat16),
+        "dp",
+        axis=0,
+        tiled=True,
+    )
+    cut = 2 * local_inner
+    inner_matrix = all_cols[:, :cut]
+    state_weight = all_cols[:, cut : cut + state_cols]
+    outer_weight = all_cols[:, cut + state_cols : cut + state_cols + local_inner]
+    step_weight = all_cols[:, cut + state_cols + local_inner :]
     stream = block_input.astype(jnp.float32)
     row_scale = lax.rsqrt(jnp.mean(stream * stream, -1, keepdims=True) + NORM_EPS)
     unit_rows = stream * row_scale
@@ -208,7 +405,6 @@
     length = seq_rows.shape[1]
     row_count = sequence_count * length
     flat_rows = seq_rows.reshape(row_count, model_width)
-    inner_matrix = inner_weight.reshape(model_width, 2 * local_inner)
     mixed_cols = matmul(flat_rows, inner_matrix)
     gate_raw = mixed_cols[:, :local_inner].reshape(sequence_count, length, local_inner)
     inner_raw = mixed_cols[:, local_inner:].reshape(sequence_count, length, local_inner)
@@ -221,11 +417,13 @@
         channel_params[: taps_count + 1],
         state_filter,
     )
-    rounded_inner = lax.optimization_barrier(active_inner.astype(jnp.bfloat16)).astype(jnp.float32)
-    rounded_state = lax.optimization_barrier(active_state.astype(jnp.bfloat16)).astype(jnp.float32)
-    gated_out, mixer_back = jax.vjp(
-        partial(mixer_part, segment), rounded_inner, rounded_state, step_raw, gate_raw, head_params
-    )
+    low_inner = lax.optimization_barrier(active_inner.astype(jnp.bfloat16))
+    low_state = lax.optimization_barrier(active_state.astype(jnp.bfloat16))
+    marks, seg_rows = segment_marks(segment)
+    mixed, saved = scan_forward(low_inner, low_state, step_raw, marks, seg_rows, head_params)
+    gate_open = jax.nn.sigmoid(gate_raw)
+    gate_silu = gate_raw * gate_open
+    gated_out = mixed * gate_silu
     squares = lax.psum(jnp.sum(gated_out * gated_out, -1), "tensor")
     inverse = lax.rsqrt(squares / (local_inner * tensor_size) + NORM_EPS)[..., None]
     gate_gain = channel_params[taps_count + 1]
@@ -233,12 +431,14 @@
     summed_parts = contract_last(normed_out.reshape(row_count, local_inner), outer_weight).reshape(
         sequence_count, length, model_width
     )
-    own_out = lax.psum_scatter(summed_parts, "tensor", scatter_dimension=1, tiled=True)
-    block_output = stream + own_out
+    own_out = lax.psum_scatter(
+        summed_parts.astype(jnp.bfloat16), "tensor", scatter_dimension=1, tiled=True
+    ).astype(jnp.float32)
     back_rows = lax.all_gather(output_grad, "tensor", axis=1, tiled=True).reshape(
         row_count, model_width
     )
     outer_grad = contract_rows(back_rows, normed_out.reshape(row_count, local_inner))
+    outer_sum = lax.psum_scatter(outer_grad, "dp", scatter_dimension=0, tiled=True)
     normed_grad = matmul(back_rows, outer_weight).reshape(sequence_count, length, local_inner)
     scaled_grad = normed_grad * gate_gain
     dot_sums = lax.psum(jnp.sum(scaled_grad * gated_out, -1), "tensor")[..., None]
@@ -246,26 +446,40 @@
         local_inner * tensor_size
     )
     gain_grad = jnp.sum(normed_grad * gated_out * inverse, axis=(0, 1))
-    inner_back, state_back, step_back, gate_back, head_grad = mixer_back(gated_grad)
-    state_total = lax.psum(state_back, "tensor")
+    dy = gated_grad * gate_silu
+    gate_back = gated_grad * mixed * (gate_open * (1.0 + gate_raw * (1.0 - gate_open)))
+    inner_back, state_back, step_back, skip_sums, small_sums = scan_backward(
+        low_inner, low_state, step_raw, marks, seg_rows, head_params, mixed, dy, saved
+    )
+    inner_back, own_out, outer_sum = lax.optimization_barrier((inner_back, own_out, outer_sum))
+    block_output = stream + own_out
+    head_grad = jnp.concatenate(
+        [
+            jnp.sum(small_sums[:, :2], 0),
+            jnp.sum(skip_sums[:, 0].reshape(sequence_count, heads_here, -1), (0, 2))[None],
+        ],
+        0,
+    )
+    state_total = lax.psum(state_back.astype(jnp.bfloat16), "tensor").astype(jnp.float32)
     inner_pre, state_pre, taps_grad, filter_grad = filter_back((inner_back, state_total))
     both_low = jnp.concatenate([gate_back.astype(jnp.bfloat16), inner_pre.astype(jnp.bfloat16)], -1)
     step_low = step_back.astype(jnp.bfloat16)
     state_low = state_pre.astype(jnp.bfloat16)
-    inner_grad = contract_rows(flat_rows, both_low.reshape(row_count, 2 * local_inner)).reshape(
-        model_width, 2, local_inner
-    )
-    step_grad = contract_rows(flat_rows, step_low.reshape(row_count, heads_here))
-    state_grad = contract_rows(flat_rows, state_low.reshape(row_count, state_cols))
+    wide_low = jnp.concatenate([both_low, state_low, step_low], -1).reshape(row_count, -1)
+    wide_grad = contract_rows(flat_rows, wide_low)
+    wide_sum = lax.psum_scatter(wide_grad, "dp", scatter_dimension=0, tiled=True)
+    inner_sum = wide_sum[:, :cut].reshape(-1, 2, local_inner)
+    state_sum = wide_sum[:, cut : cut + state_cols]
+    step_sum = wide_sum[:, cut + state_cols :]
     summed_grads = contract_last(
         both_low.reshape(row_count, 2 * local_inner), inner_matrix
     ) + contract_last(step_low.reshape(row_count, heads_here), step_weight)
     own_grad = lax.psum_scatter(
-        summed_grads.reshape(sequence_count, length, model_width),
+        summed_grads.reshape(sequence_count, length, model_width).astype(jnp.bfloat16),
         "tensor",
         scatter_dimension=1,
         tiled=True,
-    )
+    ).astype(jnp.float32)
     own_state = lax.dynamic_slice_in_dim(state_low, tensor_rank * quarter, quarter, 1)
     own_grad = own_grad + contract_last(own_state, state_weight)
     scaled_in = own_grad * input_gain
@@ -273,12 +487,6 @@
         scaled_in - unit_rows * jnp.mean(scaled_in * unit_rows, -1, keepdims=True)
     )
     input_gain_grad = jnp.sum(own_grad * unit_rows, axis=(0, 1))
-    inner_sum, step_sum, state_sum, outer_sum = (
-        lax.psum_scatter(inner_grad, "dp", scatter_dimension=0, tiled=True),
-        lax.psum_scatter(step_grad, "dp", scatter_dimension=0, tiled=True),
-        lax.psum_scatter(state_grad, "dp", scatter_dimension=0, tiled=True),
-        lax.psum_scatter(outer_grad, "dp", scatter_dimension=0, tiled=True),
-    )
     channel_grad = jnp.concatenate([taps_grad, gain_grad[None, :]], 0)
     wide_channel = lax.dynamic_update_slice(
         jnp.zeros((channel_grad.shape[0], local_inner * tensor_size), jnp.float32),

time: 2010 us -> 738 us (0.37)
  local copies, waits for them, and re-layouts: 590 us -> 30 us
  other arithmetic: 403 us -> 112 us
  matrix products: 355 us -> 68.4 us
  Pallas kernels: 0 us -> 106 us
  blocking collectives: 158 us -> 66.8 us
  waiting for transfers between devices: 422 us -> 335 us
  loops' own time: 46.8 us -> 0 us
    dynamic_update_slice x80 -> x0, local copies, waits for them, and re-layouts: 331 us -> none  [scan_states(): lax.scan(step_fn, start, (split_blocks(inputs_x), split_blocks(inputs_b),...]
    dot_general x224 -> x0, matrix products: 276 us -> none  [the longest x48 112 us: span_step(): inner_part = jnp.einsum('hts,shp->thp', weights, block_x, precision=HIGHEST)]
    reduce_scatter x4 -> x1, waiting for transfers between devices: 249 us -> 58.2 us  [shards(): lax.psum_scatter(summed_parts.astype(jnp.bfloat16), 'tensor', scatter_dim...]
    another operation x130 -> x5, other arithmetic: 182 us -> 3.59 us
    unnamed x11 -> x10, waiting for transfers between devices: 6.38 us -> 113 us
    pallas_call x0 -> x2, Pallas kernels: none -> 106 us  [the longest x1 66.6 us: scan_backward(): pl.pallas_call(partial(back_kernel, heads, inner // heads), grid=(count,...]
    all_gather x3 -> x0, blocking collectives: 91.6 us -> none  [the longest x1 33.1 us: shards(): lax.all_gather(state_proj.astype(jnp.bfloat16), 'dp', axis=0, tiled=True)]
    reduce_scatter x1, waiting for transfers between devices: 96.6 us -> 43.5 us  [shards(): lax.psum_scatter(summed_grads.reshape(sequence_count, length, model_width...]
  transfers between devices with their start and end apart: 10 -> 8, of which waited for: 8 -> 7; matrix products, arithmetic and copies ran while one was open for 30% -> 15% of each run, Pallas kernels for 0% -> 5%
where the time goes in v1:
time: 738 us; the launch traced here: 734 us
  waiting for transfers between devices  335 us (45%)
  other arithmetic  112 us (15%)
  Pallas kernels  106 us (14%)
  matrix products  68.4 us (9%)
  blocking collectives  66.8 us (9%)
  local copies, waits for them, and re-layouts  30 us (4%)
  between operations  15.1 us (2%)
    unnamed x10, waiting for transfers between devices  113 us
    pallas_call x1, Pallas kernels, scan_backward(): pl.pallas_call(partial(back_kernel, heads, inner // heads), grid=(count,...  66.6 us
    reduce_scatter x1, waiting for transfers between devices, shards(): lax.psum_scatter(summed_parts.astype(jnp.bfloat16), 'tensor', scatter_dim...  58.2 us
    all_gather x1, waiting for transfers between devices, shards(): lax.all_gather(normed, 'tensor', axis=1, tiled=True)  47.1 us
    reduce_scatter x1, waiting for transfers between devices, shards(): lax.psum_scatter(summed_grads.reshape(sequence_count, length, model_width...  43.5 us
    all_gather x1, waiting for transfers between devices, shards(): lax.all_gather(jnp.concatenate([inner_proj.reshape(-1, 2 * local_inner),...  40.3 us
    psum x1, blocking collectives, shards(): lax.psum((wide_channel, wide_head, filter_grad * leader, input_gain_grad)...  40 us
    pallas_call x1, Pallas kernels, scan_forward(): pl.pallas_call(partial(scan_kernel, heads, inner // heads), grid=(count,...  39.3 us
  transfers between devices with their start and end apart: 8, of which 7 were waited for; matrix products, arithmetic and copies ran while one was open for 15% of the time, Pallas kernels for 5%

profile of v1, /device:TPU:0, one launch (start us, length us, event | category | flops | bytes accessed | tf_op | source)
XLA Modules:
  0.0 733.9 jit_solution(2280424929311640132)
XLA Ops:
  11.8 1.8 fusion.57
  13.7 3.0 fusion.51
  17.5 6.2 all_gather.14
  24.8 1.5 pad.141.clone
  26.4 40.3 %all-gather.6.cloned.1.call-done = bf16[768,1414]{1,0:T(8,128)(2,1)} async-done(((bf16[96,1414]{1,0:T(8,128)(2,1)}), bf16[768,1414]{1,0:T(8,128)(2,1)}) %all-gather.6.cloned.1.call-update) | async-done | bytes 2171920 | tf_op jit(solution)/shard_map/all_gather | solution.py:378
  66.7 47.1 %all-gather.4.cloned.1.call-done = bf16[1,4096,768]{2,1,0:T(8,128)(2,1)} async-done(((bf16[1,1024,768]{2,1,0:T(8,128)(2,1)}), bf16[1,4096,768]{2,1,0:T(8,128)(2,1)}) %all-gather.4.cloned.1.call-update) | async-done | bytes 6291472 | tf_op jit(solution)/shard_map/all_gather | solution.py:402
  113.8 4.9 fusion.29
  118.7 5.8 multiply_convert_fusion.2
  124.5 5.1 fusion.31
  130.1 4.1 copy-done.5
  134.2 8.3 %multiply_convert_fusion.1 = (bf16[1,4096,384]{2,1,0:T(8,128)(2,1)}, f32[1,4096,384]{2,1,0:T(8,128)}) fusion(f32[4096]{0:T(1024)S(1)} %bitcast.156, f32[1,4096,384]{2,1,0:T(8,128)S(1)} %slice_bitcast_fusion, f32[384]{0:T(512)S(1)} %get-tuple-element.165, f32[4096]{0:T(1024)S(1)} %bitcast.162, f32[384]{0:T(512)S(1)} %get-tuple-element.166, ...), kind=kLoop, calls=%fused_computation.61 | loop fusion | flops 25165824 | bytes 22076928 | tf_op jit(solution)/shard_map/convert_element_type | solution.py:420
  142.4 1.9 fusion.36.step_ref
  144.3 39.3 %scan_forward.1 = (f32[1,4096,384]{2,1,0:T(8,128)}, f32[1,16,128,384]{3,2,1,0:T(8,128)}) custom-call(bf16[1,4096,384]{2,1,0:T(8,128)(2,1)} %get-tuple-element.204.x_ref, bf16[1,4096,256]{2,1,0:T(8,128)(2,1)S(1)} %get-tuple-element.202.bc_ref, f32[1,4096,6]{2,1,0:T(8,128)S(1)} %fusion.36.step_ref, f32[1,4096,8]{2,1,0:T(8,128)} %bitcast.146, ...), custom_call_target="tpu_custom_call" | custom-call | tf_op jit(solution)/shard_map/scan_forward/pallas_call | solution.py:265
  183.6 7.3 multiply_reduce_fusion.4
  190.9 10.5 %psum.49 = f32[1,4096]{1,0:T(1,128)S(1)} all-reduce(f32[1,4096]{1,0:T(1,128)S(1)} %bitcast.177), channel_id=1, replica_groups=mesh['dp'=8,'tensor'=4] {'tensor'}, use_global_device_ids=true, to_apply=%region_2.3 | all-reduce | flops 4096 | bytes 32768 | tf_op jit(solution)/shard_map/psum | solution.py:427
  201.4 8.8 %fusion.17 = (f32[384]{0:T(512)S(1)}, f32[4096]{0:T(1024)S(1)}, f32[384,4096]{0,1:T(8,128)}) fusion(f32[1,4096,384]{2,1,0:T(8,128)} %get-tuple-element.201, f32[4096]{0:T(1024)S(1)} %bitcast.173, f32[384]{0:T(512)S(1)} %get-tuple-element.164, bf16[768,1414]{1,0:T(8,128)(2,1)} %all-gather.6.cloned.1.call-done, ...), kind=kOutput, calls=%fused_computation.29 | convolution fusion | flops 2425351680 | bytes 19500032 | tf_op jit(solution)/shard_map/dot_general | solution.py:25
  210.2 10.1 %psum.50 = f32[4096]{0:T(1024)S(1)} all-reduce(f32[4096]{0:T(1024)S(1)} %get-tuple-element.154), channel_id=1, replica_groups=mesh['dp'=8,'tensor'=4] {'tensor'}, use_global_device_ids=true, to_apply=%region_4.5 | all-reduce | flops 4096 | bytes 32768 | tf_op jit(solution)/shard_map/psum | solution.py:444
  220.3 14.0 %fusion.18 = (bf16[1,4096,384]{2,1,0:T(8,128)(2,1)}, f32[1,4096,384]{2,1,0:T(8,128)}) fusion(f32[1,4096,384]{2,1,0:T(8,128)} %get-tuple-element.36.y_ref, f32[4096,768]{1,0:T(8,128)} %copy-done.5, f32[4096]{0:T(1024)S(1)} %psum.50, f32[1,4096,384]{2,1,0:T(8,128)} %get-tuple-element.201, f32[384,4096]{0,1:T(8,128)} %get-tuple-element.226, ...), kind=kLoop, calls=%fused_computation.31 | loop fusion | flops 28311552 | bytes 34653696 | tf_op jit(solution)/shard_map/convert_element_type | solution.py:465
  234.3 66.6 %scan_backward.1 = (f32[1,4096,384]{2,1,0:T(8,128)}, f32[1,4096,256]{2,1,0:T(8,128)}, f32[1,4096,6]{2,1,0:T(8,128)S(1)}, f32[1,8,384]{2,1,0:T(8,128)S(1)}, f32[1,8,6]{2,1,0:T(8,128)S(1)}) custom-call(bf16[1,4096,384]{2,1,0:T(8,128)(2,1)} %get-tuple-element.204.x_ref, bf16[1,4096,256]{2,1,0:T(8,128)(2,1)S(1)} %get-tuple-element.202.bc_ref, ...), custom_call_target="tpu_custom_call" | custom-call | tf_op jit(solution)/shard_map/scan_backward/pallas_call | solution.py:284
  302.2 3.7 convert_element_type.139
  306.0 7.4 %fusion.59 = f32[768,384]{0,1:T(8,128)S(1)} fusion(bf16[1,4096,768]{2,1,0:T(8,128)(2,1)} %all-gather.8.cloned.1.call-done, f32[1,4096,384]{2,1,0:T(8,128)} %get-tuple-element.201, f32[384]{0:T(512)S(1)} %get-tuple-element.164, f32[4096]{0:T(1024)S(1)} %bitcast.175), kind=kOutput, calls=%fused_computation.112 | convolution fusion | flops 2420637696 | bytes 13780480 | tf_op jit(solution)/shard_map/dot_general | solution.py:29
  315.1 9.1 %fusion.34 = bf16[1,4096,768]{2,1,0:T(8,128)(2,1)} fusion(bf16[768,1414]{1,0:T(8,128)(2,1)} %all-gather.6.cloned.1.call-done, f32[1,4096,384]{2,1,0:T(8,128)} %get-tuple-element.201, f32[384]{0:T(512)S(1)} %get-tuple-element.164, f32[4096]{0:T(1024)S(1)} %bitcast.176), kind=kOutput, calls=%fused_computation.63 | convolution fusion | flops 2423783424 | bytes 13190656 | tf_op jit(solution)/shard_map/dot_general | solution.py:35
  324.2 1.5 copy-done.2
  325.8 32.8 %all-reduce.32.cloned.1.call-done = bf16[1,4096,256]{2,1,0:T(8,128)(2,1)} async-done(((bf16[1,4096,256]{2,1,0:T(8,128)(2,1)}), bf16[1,4096,256]{2,1,0:T(8,128)(2,1)}) %all-reduce.32.cloned.1.call-update) | async-done | bytes 2097168 | tf_op jit(solution)/shard_map/psum | solution.py:463
  358.7 11.5 %multiply_reduce_fusion.8 = (f32[256]{0:T(256)S(1)}, f32[256]{0:T(256)S(1)}, f32[256]{0:T(256)S(1)}, f32[256]{0:T(256)S(1)}, f32[256]{0:T(256)S(1)}, /*index=5*/f32[1,4096,256]{2,1,0:T(8,128)S(1)}) fusion(f32[1,4096,256]{2,1,0:T(8,128)} %bitcast.141, f32[4096]{0:T(1024)S(1)} %bitcast.157, f32[4096]{0:T(1024)S(1)} %bitcast.163, f32[4096]{0:T(1024)S(1)} %bitcast.151, ...), kind=kLoop, calls=%fused_computation.97 | loop fusion | flops 23067392 | bytes 18928640 | tf_op jit(solution)/shard_map/transpose(jvp())/reduce_sum | solution.py:49
  370.2 1.9 multiply_multiply_fusion.3
  372.1 1.5 fusion.46
  373.7 52.8 %reduce-scatter.13.cloned.1.call-done = f32[96,384]{1,0:T(8,128)} async-done(((f32[768,384]{1,0:T(8,128)}), f32[96,384]{1,0:T(8,128)}) %reduce-scatter.13.cloned.1.call-update) | async-done | bytes 147472
  426.4 1.7 copy.155
  428.1 58.2 %reduce-scatter.9.cloned.1.call-done = bf16[1,1024,768]{2,1,0:T(8,128)(2,1)} async-done(((bf16[1,4096,768]{2,1,0:T(8,128)(2,1)}), bf16[1,1024,768]{2,1,0:T(8,128)(2,1)}) %reduce-scatter.9.cloned.1.call-update) | async-done | bytes 1572880 | tf_op jit(solution)/shard_map/reduce_scatter | solution.py:434
  486.4 3.3 convert_element_type.131
  489.7 16.5 %multiply_reduce_fusion.3 = (f32[384]{0:T(512)S(1)}, f32[384]{0:T(512)S(1)}, f32[384]{0:T(512)S(1)}, f32[384]{0:T(512)S(1)}, f32[384]{0:T(512)S(1)}, /*index=5*/f32[1,4096,384]{2,1,0:T(8,128)S(1)}) fusion(f32[1,4096,384]{2,1,0:T(8,128)} %copy-done.6, f32[4096]{0:T(1024)S(1)} %bitcast.159, f32[4096]{0:T(1024)S(1)} %bitcast.165, f32[4096]{0:T(1024)S(1)} %bitcast.153, ...), kind=kLoop, calls=%fused_computation.55 | loop fusion | flops 33028224 | bytes 31514112 | tf_op jit(solution)/shard_map/transpose(jvp())/reduce_sum | solution.py:49
  506.2 5.6 multiply_multiply_fusion
  511.8 7.8 %fusion.10 = bf16[1,4096,384]{2,1,0:T(8,128)(2,1)} fusion(f32[1,4096,384]{2,1,0:T(8,128)} %get-tuple-element.210, f32[1,4096,384]{2,1,0:T(8,128)} %get-tuple-element.209, f32[1,4096,384]{2,1,0:T(8,128)S(1)} %get-tuple-element.208, f32[1,4096,384]{2,1,0:T(8,128)S(1)} %get-tuple-element.187, f32[384]{0:T(512)S(1)} %get-tuple-element.168), kind=kLoop, calls=%fused_computation.20 | loop fusion | flops 7864320 | bytes 28313088 | tf_op jit(solution)/shard_map/convert_element_type | solution.py:465
  519.6 13.4 %fusion = f32[768,1030]{1,0:T(8,128)} fusion(bf16[1,4096,6]{2,1,0:T(8,128)(2,1)S(1)} %convert_element_type.135, bf16[1,4096,256]{2,1,0:T(8,128)(2,1)S(1)} %fusion.46, bf16[1,4096,384]{2,1,0:T(8,128)(2,1)} %fusion.10, bf16[1,4096,384]{2,1,0:T(8,128)(2,1)} %get-tuple-element.206, bf16[1,4096,768]{2,1,0:T(8,128)(2,1)S(1)} %bitcast.145), kind=kOutput, calls=%fused_computation.3 | convolution fusion | flops 6513950720 | bytes 17893376
  533.1 7.9 %fusion.13 = f32[4096,768]{1,0:T(8,128)S(1)} fusion(bf16[1,4096,384]{2,1,0:T(8,128)(2,1)} %fusion.10, bf16[1,4096,384]{2,1,0:T(8,128)(2,1)} %get-tuple-element.206, bf16[768,1414]{1,0:T(8,128)(2,1)} %all-gather.6.cloned.1.call-done), kind=kOutput, calls=%fused_computation.24 | convolution fusion | flops 4844421120 | bytes 20054016 | tf_op jit(solution)/shard_map/dot_general | solution.py:35
  541.0 5.5 fusion.35
  553.0 59.3 %reduce-scatter.15.cloned.1.call-done = f32[96,1030]{1,0:T(8,128)} async-done(((f32[768,1030]{1,0:T(8,128)}), f32[96,1030]{1,0:T(8,128)}) %reduce-scatter.15.cloned.1.call-update) | async-done | bytes 395536
  614.3 1.7 multiply_subtract_fusion.2
  617.5 1.8 copy.145
  619.2 1.8 slice.161
  621.0 1.9 copy.159
  622.9 2.0 copy.134
  626.3 3.1 multiply_subtract_fusion
  629.3 43.5 %reduce-scatter.11.cloned.1.call-done = bf16[1,1024,768]{2,1,0:T(8,128)(2,1)} async-done(((bf16[1,4096,768]{2,1,0:T(8,128)(2,1)}), bf16[1,1024,768]{2,1,0:T(8,128)(2,1)}) %reduce-scatter.11.cloned.1.call-update) | async-done | bytes 1572880 | tf_op jit(solution)/shard_map/reduce_scatter | solution.py:477
  672.9 4.6 fusion.56
  677.5 40.0 %all-reduce.29 = (f32[6,1536]{1,0:T(8,128)S(1)}, f32[3,24]{1,0:T(4,128)S(1)}, f32[5,256]{1,0:T(8,128)S(1)}, f32[768]{0:T(1024)S(1)}) all-reduce(f32[6,1536]{1,0:T(8,128)S(1)} %maximum_dynamic-update-slice_fusion, f32[3,24]{1,0:T(4,128)} %copy-done.31, ...), channel_id=1, replica_groups=mesh['dp'=8,'tensor'=4] {'dp','tensor'}, use_global_device_ids=true, to_apply=%region_17.18 | all-reduce | flops 11336 | bytes 90688 | tf_op jit(solution)/shard_map/psum | solution.py:502
  718.2 6.7 fusion.55
  (165 shorter events, 24.0 us)
Async XLA Ops:
  7.2 10.2 %copy-start.32 = (s32[1,1024]{1,0:T(1,128)S(1)}, s32[1,1024]{1,0:T(1,128)}, u32[]{:S(2)}) copy-start(s32[1,1024]{1,0:T(1,128)} %param.29) | copy-start | bytes 12292
  7.2 59.5 %all-gather.6.cloned.1.call-start = ((), (), s32[]{:S(2)}) async-start(), calls=%async_computation.5 | async-start | bytes 2654208 | tf_op jit(solution)/shard_map/all_gather | solution.py:378
  11.8 102.0 %all-gather.4.cloned.1.call-start = ((), (), s32[]{:S(2)}) async-start(), calls=%async_computation.4 | async-start | bytes 7864320 | tf_op jit(solution)/shard_map/all_gather | solution.py:402
  13.6 12.7 %copy-start.22 = (f32[1024]{0:T(1024)}, f32[1024]{0:T(1024)S(1)}, u32[]{:S(2)}) copy-start(f32[1024]{0:T(1024)S(1)} %add_rsqrt_fusion.1) | copy-start | bytes 12292
  13.6 12.7 %copy-start.19 = (f32[6,384]{1,0:T(8,128)S(1)}, f32[6,384]{1,0:T(8,128)}, u32[]{:S(2)}) copy-start(f32[6,384]{1,0:T(8,128)} %param.42) | copy-start | bytes 27652
  13.6 12.8 %copy-start.24 = (f32[5,256]{1,0:T(8,128)S(1)}, f32[5,256]{1,0:T(8,128)}, u32[]{:S(2)}) copy-start(f32[5,256]{1,0:T(8,128)} %param.48) | copy-start | bytes 15364
  16.7 184.8 %all-gather.8.cloned.1.call-start = ((), (), s32[]{:S(2)}) async-start(), calls=%async_computation.6 | async-start | bytes 7864320 | tf_op jit(solution)/shard_map/all_gather | solution.py:437
  17.4 341.3 %all-reduce.32.cloned.1.call-start = ((), (), s32[]{:S(2)}) async-start(), calls=%async_computation.9 | async-start | bytes 4194304 | tf_op jit(solution)/shard_map/psum | solution.py:463
  113.8 10.7 %slice-start = ((s8[6291456]{0:T(1024)(128)(4,1)}), s8[4194304]{0:T(1024)(128)(4,1)S(1)}, s32[]{:S(2)}) async-start(s8[6291456]{0:T(1024)(128)(4,1)} %bitcast.142), calls=%async_computation.12 | async-start | bytes 8388608
  118.7 5.8 copy-start.4
  118.7 5.8 slice-start.1
  118.7 5.8 copy-start.14
  129.6 4.6 copy-start.5
  130.0 12.4 %copy-start.6 = (f32[1,4096,384]{2,1,0:T(8,128)}, f32[1,4096,384]{2,1,0:T(8,128)S(1)}, u32[]{:S(2)}) copy-start(f32[1,4096,384]{2,1,0:T(8,128)S(1)} %slice_bitcast_fusion) | copy-start | bytes 18874372
  142.4 1.9 copy-start.3
  144.3 46.6 %copy-start = (f32[1,4096,6]{2,1,0:T(8,128)}, f32[1,4096,6]{2,1,0:T(8,128)S(1)}, u32[]{:S(2)}) copy-start(f32[1,4096,6]{2,1,0:T(8,128)S(1)} %fusion.36.step_ref) | copy-start | bytes 294916
  300.9 1.3 copy-start.1
  305.9 120.5 %reduce-scatter.13.cloned.1.call-start = ((), (), s32[]{:S(2)}) async-start(), calls=%async_computation.10 | async-start | bytes 1327104
  314.8 171.6 %reduce-scatter.9.cloned.1.call-start = ((), (), s32[]{:S(2)}) async-start(), calls=%async_computation.7 | async-start | bytes 7864320 | tf_op jit(solution)/shard_map/reduce_scatter | solution.py:434
  324.1 1.6 copy-start.2
  324.1 288.2 %reduce-scatter.15.cloned.1.call-start = ((), (), s32[]{:S(2)}) async-start(), calls=%async_computation.11 | async-start | bytes 3981312
  373.7 145.9 %copy-start.9 = (bf16[1,4096,256]{2,1,0:T(8,128)(2,1)}, bf16[1,4096,256]{2,1,0:T(8,128)(2,1)S(1)}, u32[]{:S(2)}) copy-start(bf16[1,4096,256]{2,1,0:T(8,128)(2,1)S(1)} %fusion.46) | copy-start | bytes 6291460
  506.2 13.4 %slice-start.2 = ((s8[6291456]{0:T(1024)(128)(4,1)}), s8[4194304]{0:T(1024)(128)(4,1)S(1)}, s32[]{:S(2)}) async-start(s8[6291456]{0:T(1024)(128)(4,1)} %bitcast.144), calls=%async_computation.14 | async-start | bytes 8388608
  511.8 7.8 %slice-start.3 = ((s8[6291456]{0:T(1024)(128)(4,1)}), s8[2097152]{0:T(1024)(128)(4,1)S(1)}, s32[]{:S(2)}) async-start(s8[6291456]{0:T(1024)(128)(4,1)} %bitcast.144), calls=%async_computation.15 | async-start | bytes 4194304
  533.0 139.8 %reduce-scatter.11.cloned.1.call-start = ((), (), s32[]{:S(2)}) async-start(), calls=%async_computation.8 | async-start | bytes 7864320 | tf_op jit(solution)/shard_map/reduce_scatter | solution.py:477
  546.5 0.9 copy-start.13
  546.5 1.0 copy-start.12
  546.5 1.1 copy-start.17
  546.5 1.9 copy-start.18
  546.5 2.7 copy-start.15
  546.5 2.8 copy-start.16
  546.5 3.9 copy-start.11
  546.5 78.4 %copy-start.26 = (f32[96,6]{0,1:T(8,128)S(1)}, f32[96,6]{0,1:T(8,128)}, u32[]{:S(2)}) copy-start(f32[96,6]{0,1:T(8,128)} %param.33) | copy-start | bytes 6916
  546.5 79.7 %copy-start.10 = (f32[96,2,384]{2,1,0:T(2,128)S(1)}, f32[96,2,384]{2,1,0:T(2,128)}, u32[]{:S(2)}) copy-start(f32[96,2,384]{2,1,0:T(2,128)} %param.30) | copy-start | bytes 884740
  546.6 126.3 %copy-start.7 = (bf16[1,1024,768]{2,1,0:T(8,128)(2,1)S(1)}, bf16[1,1024,768]{2,1,0:T(8,128)(2,1)}, u32[]{:S(2)}) copy-start(bf16[1,1024,768]{2,1,0:T(8,128)(2,1)} %param.27) | copy-start | bytes 4718596
  546.6 126.3 %copy-start.21 = (f32[768]{0:T(1024)S(1)}, f32[768]{0:T(1024)}, u32[]{:S(2)}) copy-start(f32[768]{0:T(1024)} %param.51) | copy-start | bytes 9220
  546.6 126.3 %copy-start.23 = (f32[1024]{0:T(1024)S(1)}, f32[1024]{0:T(1024)}, u32[]{:S(2)}) copy-start(f32[1024]{0:T(1024)} %copy-done.22) | copy-start | bytes 12292
  617.5 100.1 %copy-start.20 = (f32[6,384]{1,0:T(8,128)S(1)}, f32[6,384]{1,0:T(8,128)}, u32[]{:S(2)}) copy-start(f32[6,384]{1,0:T(8,128)} %param.42) | copy-start | bytes 27652
  617.5 100.1 %copy-start.27 = (f32[6,384]{1,0:T(8,128)S(1)}, f32[6,384]{1,0:T(8,128)}, u32[]{:S(2)}) copy-start(f32[6,384]{1,0:T(8,128)} %param.44) | copy-start | bytes 27652
  617.5 100.1 %copy-start.28 = (f32[6,384]{1,0:T(8,128)S(1)}, f32[6,384]{1,0:T(8,128)}, u32[]{:S(2)}) copy-start(f32[6,384]{1,0:T(8,128)} %param.43) | copy-start | bytes 27652
  617.5 100.7 %copy-start.8 = (bf16[1,1024,768]{2,1,0:T(8,128)(2,1)S(1)}, bf16[1,1024,768]{2,1,0:T(8,128)(2,1)}, u32[]{:S(2)}) copy-start(bf16[1,1024,768]{2,1,0:T(8,128)(2,1)} %param.28) | copy-start | bytes 4718596
  718.2 6.8 copy-start.35
  718.2 6.8 copy-start.36
  718.2 7.4 %copy-start.33 = (f32[768]{0:T(1024)S(1)}, f32[768]{0:T(1024)}, u32[]{:S(2)}) copy-start(f32[768]{0:T(1024)} %param.53) | copy-start | bytes 9220
  718.2 7.4 %copy-start.34 = (f32[768]{0:T(1024)S(1)}, f32[768]{0:T(1024)}, u32[]{:S(2)}) copy-start(f32[768]{0:T(1024)} %param.52) | copy-start | bytes 9220
  718.2 8.0 %copy-start.25 = (f32[5,256]{1,0:T(8,128)S(1)}, f32[5,256]{1,0:T(8,128)}, u32[]{:S(2)}) copy-start(f32[5,256]{1,0:T(8,128)} %param.48) | copy-start | bytes 15364
  718.2 8.0 %copy-start.29 = (f32[5,256]{1,0:T(8,128)S(1)}, f32[5,256]{1,0:T(8,128)}, u32[]{:S(2)}) copy-start(f32[5,256]{1,0:T(8,128)} %param.50) | copy-start | bytes 15364
  718.2 8.0 %copy-start.30 = (f32[5,256]{1,0:T(8,128)S(1)}, f32[5,256]{1,0:T(8,128)}, u32[]{:S(2)}) copy-start(f32[5,256]{1,0:T(8,128)} %param.49) | copy-start | bytes 15364
  (1 other events, 0.6 us)
Sparse Core Ops, SparseCore 0:
  11.9 54.7 all-gather.5
  68.8 44.8 all-gather.3
  115.3 46.3 all-gather.7
  306.1 52.5 all-reduce.31
  362.3 64.0 reduce-scatter.12
  429.0 57.3 reduce-scatter.8
  533.2 79.1 reduce-scatter.14
  614.9 57.8 reduce-scatter.10
